TPU v7x, 256 devices: a whole 4x4x8 slice. The times are simulated.
256 devices in a mesh: wide: 32 (over x, z_hi, y), narrow: 8 (over z_lo, core).
Axes of the slice: x: 4, y: 4, z: 8 (z_hi: 2, z_lo: 4; z = z_hi * 4 + z_lo), core: 2. Of those that a mesh axis runs over, the one named last changes fastest.
Arguments:
- amplitudes: bfloat16 [65536, 1024], P('wide', 'narrow'), may hold values from -6 to 6
- pair_mask: int32 [512, 8], P('wide', 'narrow'), may hold values 0 or 1
- integrals: bfloat16 [1024, 16384], P('wide', 'narrow'), may hold values from -0.1875 to 0.1875
Outputs:
- ladder: bfloat16 [65536, 16384], P('wide', 'narrow')
All inputs are finite; a program needn't handle non-finite values. No bound on the sum of `pair_mask` on one device may be relied on, other than what follows from the above.
Results may differ from a plain program's by a relative error of at most 0.001.
Values may be sent and summed in bfloat16 or wider, within the bound.
A program may use at most 64 MiB of HBM per device.

v0:
```python
import jax
import jax.numpy as jnp
from jax import lax
from jax.sharding import Mesh
from jax.sharding import PartitionSpec as P

VB = 128
NARROW = ("narrow_0", "narrow_1")
WIDE = ("wide_0", "wide_1", "wide_2")


def sent_to_all(shard, axis):
    length = lax.axis_size(axis)
    return lax.all_to_all(
        jnp.broadcast_to(shard[None], (length, *shard.shape)), axis, 0, 0, tiled=True
    )


def laid_out(tiles, dim):
    tiles = jnp.moveaxis(tiles, 0, dim)
    shape = tiles.shape
    return tiles.reshape(*shape[:dim], shape[dim] * shape[dim + 1], *shape[dim + 2 :])


def gather_axes(shard, axes, dim):
    far, near = axes
    leading = sent_to_all(shard, far)
    tiles = jnp.swapaxes(sent_to_all(leading, near), 0, 1)
    return laid_out(tiles.reshape(-1, *shard.shape), dim)


def gather_in_order(shard, axes, sequence):
    tiles = shard[None]
    for k in sequence:
        tiles = lax.all_gather(tiles, axes[k], axis=0, tiled=True)
    block = [lax.axis_size(axes[k]) for k in reversed(sequence)]
    tiles = tiles.reshape(*block, *shard.shape)
    turned = sorted(range(len(sequence)), key=lambda place: sequence[len(sequence) - 1 - place])
    return tiles.transpose(*turned, *range(len(sequence), tiles.ndim)).reshape(-1, *shard.shape)


def gathered_by_axis(shard, axes, sequence, dim):
    return laid_out(gather_in_order(shard, axes, sequence), dim)


def shards(amplitudes, pair_mask, integrals):
    tiles = jnp.repeat(jnp.repeat(pair_mask, VB, axis=0), VB, axis=1)
    masked = amplitudes * tiles.astype(jnp.bfloat16)
    whole_rows = gather_axes(masked, ("narrow_0", "narrow_1"), 1)
    result = jnp.dot(
        whole_rows,
        gathered_by_axis(integrals, WIDE, (1, 0, 2), 0),
        preferred_element_type=jnp.float32,
    )
    return result.astype(jnp.bfloat16)


def solution(mesh):
    split = Mesh(
        mesh.devices.reshape(4, 2, 4, 4, 2), ("wide_0", "wide_1", "wide_2", "narrow_0", "narrow_1")
    )
    placed = (P(WIDE, NARROW), P(WIDE, NARROW), P(WIDE, NARROW))
    return jax.shard_map(
        shards, mesh=split, in_specs=placed, out_specs=P(WIDE, NARROW), check_vma=False
    )
```

profile of v0, /device:TPU:1, one launch (start us, length us, event | category | flops | bytes accessed | tf_op | source)
XLA Modules:
  0.0 142.3 jit_solution(9726958274767241918)
XLA Ops:
  6.5 0.0 all-gather.4.cloned.1.call-start
  6.5 13.5 %all-gather = bf16[64,2048]{1,0:T(8,128)(2,1)} all-gather(bf16[32,2048]{1,0:T(8,128)(2,1)} %param.5), channel_id=2, replica_groups=mesh['wide_0'=4,'wide_1'=2,'wide_2'=4,'narrow_0'=4,'narrow_1'=2] {'wide_1'}, dimensions={0}, use_global_device_ids=true | all-gather | bytes 393216 | tf_op jit(solution)/shard_map/all_gather | solution.py:35
  20.0 0.0 all-gather.4.cloned.1.call-update
  20.0 0.0 all-gather.6.cloned.1.call-start
  20.1 28.5 %all-gather.4.cloned.1.call-done = bf16[8,32,2048]{2,1,0:T(8,128)(2,1)} async-done(((bf16[2,32,2048]{2,1,0:T(8,128)(2,1)}), bf16[8,32,2048]{2,1,0:T(8,128)(2,1)}) %all-gather.4.cloned.1.call-update) | async-done | bytes 1048592 | tf_op jit(solution)/shard_map/all_gather | solution.py:35
  48.6 0.0 all-gather.6.cloned.1.call-update
  48.6 0.7 convert_bitcast_fusion
  49.3 0.1 broadcast_bitcast_fusion
  49.4 1.4 broadcast_multiply_fusion
  50.7 0.3 broadcast_in_dim.9
  51.0 51.6 %all_to_all.10 = bf16[4,2048,128]{2,1,0:T(8,128)(2,1)S(1)} all-to-all(bf16[4,2048,128]{2,1,0:T(8,128)(2,1)S(1)} %broadcast_in_dim.9), channel_id=1, replica_groups=mesh['wide_0'=4,'wide_1'=2,'wide_2'=4,'narrow_0'=4,'narrow_1'=2] {'narro..., dimensions={0} | all-to-all | bytes 4194304 | tf_op jit(solution)/shard_map/all_to_all | solution.py:14
  102.6 0.5 broadcast_in_dim.10
  103.2 8.6 %all_to_all.11 = bf16[2,4,2048,128]{3,2,1,0:T(8,128)(2,1)S(1)} all-to-all(bf16[2,4,2048,128]{3,2,1,0:T(8,128)(2,1)S(1)} %broadcast_in_dim.10), channel_id=1, replica_groups=mesh['wide_0'=4,'wide_1'=2,'wide_2'=4,'narrow_0'=4,'narrow_1'=2] {'narro..., dimensions={0} | all-to-all | bytes 8388608 | tf_op jit(solution)/shard_map/all_to_all | solution.py:14
  111.8 2.3 %copy.7 = bf16[2,4,2048,128]{3,2,0,1:T(8,128)(2,1)} copy(bf16[2,4,2048,128]{3,2,1,0:T(8,128)(2,1)S(1)} %all_to_all.11) | data formatting | bytes 8388608 | tf_op jit(solution)/shard_map/all_to_all | solution.py:14
  114.1 6.5 %copy.8 = bf16[2048,8,128]{0,2,1:T(8,128)(2,1)} copy(bf16[2048,8,128]{2,0,1:T(8,128)(2,1)} %bitcast.17) | data formatting | bytes 8388608 | tf_op jit(solution)/shard_map/transpose | solution.py:20
  120.6 0.0 all-gather.6.cloned.1.call-done
  120.6 0.0 copy-start
  120.6 2.9 %copy.9 = bf16[4,2,4,32,2048]{4,3,2,1,0:T(8,128)(2,1)S(1)} copy(bf16[4,2,4,32,2048]{4,3,1,0,2:T(8,128)(2,1)} %bitcast.18) | data formatting | bytes 8388608 | tf_op jit(solution)/shard_map/transpose | solution.py:39
  123.5 0.6 copy-done
  124.1 11.4 %convolution_convert_fusion = bf16[2048,2048]{1,0:T(8,128)(2,1)} fusion(bf16[2048,1024]{0,1:T(8,128)(2,1)S(1)} %bitcast.19, bf16[1024,2048]{1,0:T(8,128)(2,1)S(1)} %bitcast.20), kind=kOutput, calls=%fused_computation | convolution fusion | flops 8594128896 | bytes 16777216 | tf_op jit(solution)/shard_map/dot_general | solution.py:50
Async XLA Ops:
  6.5 42.1 %all-gather.4.cloned.1.call-start = ((), (), s32[]{:S(2)}) async-start(), calls=%async_computation.2 | async-start | bytes 1310720 | tf_op jit(solution)/shard_map/all_gather | solution.py:35
  20.0 100.6 %all-gather.6.cloned.1.call-start = ((), (), s32[]{:S(2)}) async-start(), calls=%async_computation.3 | async-start | bytes 5242880 | tf_op jit(solution)/shard_map/all_gather | solution.py:35
  120.6 3.4 %copy-start = (bf16[2048,8,128]{0,2,1:T(8,128)(2,1)S(1)}, bf16[2048,8,128]{0,2,1:T(8,128)(2,1)}, u32[]{:S(2)}) copy-start(bf16[2048,8,128]{0,2,1:T(8,128)(2,1)} %copy.8) | copy-start | bytes 12582916
Sparse Core Ops, SparseCore 0:
  20.2 28.3 all-gather.3
  50.4 52.1 all-gather.5
where the time goes:
time: 143 us; the launch traced here: 142 us
  blocking collectives  73.7 us (52%)
  waiting for transfers between devices  28.5 us (20%)
  between operations  13.4 us (9%)
  local copies, waits for them, and re-layouts  13.2 us (9%)
  matrix products  11.4 us (8%)
  other arithmetic  2.04 us (1%)
    all_to_all x2, blocking collectives, sent_to_all(): lax.all_to_all(jnp.broadcast_to(shard[None], (length, *shard.shape)), axi...  60.2 us
    all_gather x2, waiting for transfers between devices, gather_in_order(): tiles = lax.all_gather(tiles, axes[k], axis=0, tiled=True)  28.5 us
    all_gather x1, blocking collectives, gather_in_order(): tiles = lax.all_gather(tiles, axes[k], axis=0, tiled=True)  13.5 us
    dot_general x1, matrix products, shards(): jnp.dot(whole_rows, gathered_by_axis(integrals, WIDE, (1, 0, 2), 0), pref...  11.4 us
    transpose x1, local copies, waits for them, and re-layouts, laid_out(): tiles = jnp.moveaxis(tiles, 0, dim)  6.52 us
    transpose x1, local copies, waits for them, and re-layouts, gather_in_order(): tiles.transpose(*turned, *range(len(sequence), tiles.ndim))  2.86 us
  transfers between devices with their start and end apart: 2, of which 1 were waited for; matrix products, arithmetic and copies ran while one was open for 8% of the time, Pallas kernels for 0%

commit v1 on v0

v1 whole, which is shorter than its diff:
```python
import functools

import jax
import jax.numpy as jnp
from jax import lax
from jax.experimental import pallas as pl
from jax.experimental.pallas import tpu as pltpu
from jax.sharding import PartitionSpec as P

MESH = pl.DeviceIdType.MESH
VB = 128
LINE = 4
RING = 4
CORES = 2
CHUNK = 128
COLS = 512
WRITES = 8


def kernel(mask_ref, a_ref, b_ref, out_ref, a_in, a_all, b_all, local, za, ca, up, down, side, zb, sb):
    wide, narrow = lax.axis_index("wide"), lax.axis_index("narrow")
    zl, core = narrow // CORES, narrow % CORES
    x, zh, y = wide // (2 * RING), (wide // RING) % 2, wide % RING
    rows, width = a_in.shape
    depth = b_ref.shape[0]
    half = depth // 2
    chunks = rows // CHUNK

    def wide_of(layer, first, second):
        px = (x + (1 - core) * first + core * second) % RING
        py = (y + core * first + (1 - core) * second) % RING
        return (px * 2 + (zh + layer) % 2) * RING + py

    other = (wide, zl * CORES + 1 - core)
    above, below = (wide, narrow + CORES), (wide, narrow - CORES)

    take_b = pltpu.make_async_copy(b_ref, b_all.at[pl.ds(wide * depth, depth)], local.at[0])
    take_a = pltpu.make_async_copy(a_ref, a_in, local.at[1])
    take_b.start()
    take_a.start()

    barrier = pltpu.get_barrier_semaphore()

    def greet(device):
        pl.semaphore_signal(barrier, inc=1, device_id=device, device_id_type=MESH)

    for first, second in ((1, 0), (3, 0), (0, 1), (0, 3)):
        greet((wide_of(0, first, second), narrow))
    greet((wide_of(1, 0, 0), narrow))
    greet(other)

    @pl.when(zl < LINE - 1)
    def _():
        greet(above)

    @pl.when(zl > 0)
    def _():
        greet(below)

    inner = jnp.where((zl > 0) & (zl < LINE - 1), 1, 0)
    pl.semaphore_wait(barrier, 7 + inner)
    take_b.wait()

    sent = []

    def b_part(layer, first, second, part):
        base = wide_of(layer, first, second) * depth
        if part is None:
            return b_all.at[pl.ds(base, depth)]
        return b_all.at[pl.ds(base + part * half, half)]

    def b_copy(layer, first, second, part, to, label):
        where = b_part(layer, first, second, part)
        return pltpu.make_async_remote_copy(
            where,
            where,
            sb.at[len(sent)],
            zb.at[label[0], label[1] % RING, label[2] % RING, part or 0],
            device_id=(wide_of(*to), narrow),
            device_id_type=MESH,
        )

    def b_send(layer, first, second, part, step):
        df, ds = step
        copy = b_copy(layer, first, second, part, (0, df, ds), (layer, first - df, second - ds))
        copy.start()
        sent.append(copy)

    def b_wait(layer, first, second, part):
        where = b_part(layer, first, second, part)
        pltpu.make_async_remote_copy(
            where,
            where,
            sb.at[0],
            zb.at[layer, first % RING, second % RING, part or 0],
            device_id=other,
            device_id_type=MESH,
        ).wait_recv()

    def b_begin(layer):
        for step in ((1, 0), (3, 0), (0, 1), (0, 3)):
            b_send(layer, 0, 0, None, step)

    def b_near(layer):
        b_wait(layer, 3, 0, None)
        b_send(layer, 3, 0, 0, (1, 0))
        b_send(layer, 3, 0, None, (0, 1))
        b_send(layer, 3, 0, None, (0, 3))
        b_wait(layer, 1, 0, None)
        b_send(layer, 1, 0, 1, (3, 0))
        b_send(layer, 1, 0, None, (0, 1))
        b_send(layer, 1, 0, None, (0, 3))

    def b_far(layer):
        b_wait(layer, 2, 0, 0)
        b_wait(layer, 2, 0, 1)
        b_send(layer, 2, 0, None, (0, 1))
        b_send(layer, 2, 0, None, (0, 3))

    def b_turn(layer, first):
        b_wait(layer, first, 3, None)
        b_send(layer, first, 3, 0, (0, 1))
        b_wait(layer, first, 1, None)
        b_send(layer, first, 1, 1, (0, 3))

    def b_end(layer):
        for first in range(RING):
            b_wait(layer, first, 2, 0)
            b_wait(layer, first, 2, 1)

    swap = b_copy(0, 0, 0, None, (1, 0, 0), (1, 0, 0))
    swap.start()
    sent.append(swap)
    b_begin(0)

    def a_copy(source, r, send, recv, device):
        where = a_all.at[source, core, pl.ds(pl.multiple_of(r * CHUNK, CHUNK), CHUNK)]
        return pltpu.make_async_remote_copy(
            where, where, send.at[source, r], recv.at[source, r], device_id=device, device_id_type=MESH
        )

    def over(source, r):
        return a_copy(source, r, side, ca, other)

    def upward(source, r):
        return a_copy(source, r, up, za, above)

    def downward(source, r):
        return a_copy(source, r, down, za, below)

    def from_other(source, r):
        where = a_all.at[source, 1 - core, pl.ds(pl.multiple_of(r * CHUNK, CHUNK), CHUNK)]
        pltpu.make_async_remote_copy(
            where, where, side.at[source, r], ca.at[source, r], device_id=other, device_id_type=MESH
        ).wait_recv()

    take_a.wait()

    def own(r, _):
        span = pl.ds(pl.multiple_of(r * CHUNK, CHUNK), CHUNK)
        keep = mask_ref[0, r * CHUNK // VB].astype(jnp.float32)
        a_all[zl, core, span, :] = (a_in[span, :].astype(jnp.float32) * keep).astype(jnp.bfloat16)

        @pl.when(zl < LINE - 1)
        def _():
            upward(zl, r).start()

        @pl.when(zl > 0)
        def _():
            downward(zl, r).start()

        over(zl, r).start()
        return 0

    lax.fori_loop(0, chunks, own, 0)

    def forward(distance, r):
        @pl.when(zl - distance >= 0)
        def _():
            upward(zl - distance, r).wait_recv()

            @pl.when(zl < LINE - 1)
            def _():
                upward(zl - distance, r).start()

            over(zl - distance, r).start()

        @pl.when(zl + distance < LINE)
        def _():
            downward(zl + distance, r).wait_recv()

            @pl.when(zl > 0)
            def _():
                downward(zl + distance, r).start()

            over(zl + distance, r).start()

    def forwards(distance, start, stop):
        def body(r, _):
            forward(distance, r)
            return 0

        lax.fori_loop(start * chunks // 16, stop * chunks // 16, body, 0)

    b_near(0)
    b_far(0)
    for first in range(RING):
        b_turn(0, first)
    forwards(1, 0, 8)
    b_wait(1, 0, 0, None)
    b_begin(1)
    forwards(1, 8, 10)
    b_near(1)
    forwards(1, 10, 12)
    b_far(1)
    forwards(1, 12, 16)
    for first in range(RING):
        b_turn(1, first)
    b_end(0)
    b_end(1)
    forwards(2, 0, 16)

    def product(r):
        span = pl.ds(pl.multiple_of(r * CHUNK, CHUNK), CHUNK)
        for source in range(LINE):
            from_other(source, r)
        left = jnp.concatenate([a_all[s, c, span, :] for s in range(LINE) for c in range(CORES)], axis=1)
        for start in range(0, out_ref.shape[1], COLS):
            out_ref[span, start : start + COLS] = jnp.dot(
                left, b_all[:, start : start + COLS], preferred_element_type=jnp.float32
            ).astype(out_ref.dtype)

    def last(r, _):
        forward(3, r)

        @pl.when(r > 0)
        def _():
            product(r - 1)

        return 0

    lax.fori_loop(0, chunks, last, 0)
    product(chunks - 1)

    for copy in sent:
        copy.wait_send()

    def finish(i, _):
        source, r = i // chunks, i % chunks
        over(source, r).wait_send()

        @pl.when((source <= zl) & (zl < LINE - 1))
        def _():
            upward(source, r).wait_send()

        @pl.when((source >= zl) & (zl > 0))
        def _():
            downward(source, r).wait_send()

        return 0

    lax.fori_loop(0, LINE * chunks, finish, 0)


def write_out(from_ref, to_ref, sem):
    size = from_ref.shape[0] // WRITES
    copies = [
        pltpu.make_async_copy(from_ref.at[pl.ds(i * size, size)], to_ref.at[pl.ds(i * size, size)], sem.at[i])
        for i in range(WRITES)
    ]
    for copy in copies:
        copy.start()
    for copy in copies:
        copy.wait()


def shards(amplitudes, pair_mask, integrals):
    rows, width = amplitudes.shape
    depth, columns = integrals.shape
    deep = depth * 2 * RING * RING
    chunks = rows // CHUNK
    dma = pltpu.SemaphoreType.DMA
    result = pl.pallas_call(
        kernel,
        out_shape=jax.ShapeDtypeStruct((rows, columns), jnp.bfloat16),
        in_specs=[
            pl.BlockSpec(memory_space=pltpu.SMEM),
            pl.BlockSpec(memory_space=pltpu.HBM),
            pl.BlockSpec(memory_space=pltpu.HBM),
        ],
        out_specs=pl.BlockSpec(memory_space=pltpu.VMEM),
        scratch_shapes=[
            pltpu.VMEM((rows, width), jnp.bfloat16),
            pltpu.VMEM((LINE, CORES, rows, width), jnp.bfloat16),
            pltpu.VMEM((deep, columns), jnp.bfloat16),
            dma((2,)),
            dma((LINE, chunks)),
            dma((LINE, chunks)),
            dma((LINE, chunks)),
            dma((LINE, chunks)),
            dma((LINE, chunks)),
            dma((2, RING, RING, 2)),
            dma((48,)),
        ],
        compiler_params=pltpu.CompilerParams(
            collective_id=0, has_side_effects=True, vmem_limit_bytes=32 * 2**20
        ),
        cost_estimate=pl.CostEstimate(
            flops=2 * rows * columns * deep, bytes_accessed=2 * rows * columns, transcendentals=0
        ),
    )(pair_mask.reshape(1, -1), amplitudes, integrals)
    return pl.pallas_call(
        write_out,
        out_shape=jax.ShapeDtypeStruct(result.shape, result.dtype),
        in_specs=[pl.BlockSpec(memory_space=pl.ANY)],
        out_specs=pl.BlockSpec(memory_space=pltpu.HBM),
        scratch_shapes=[dma((WRITES,))],
        compiler_params=pltpu.CompilerParams(vmem_limit_bytes=2**20),
        cost_estimate=pl.CostEstimate(flops=0, bytes_accessed=2 * rows * columns, transcendentals=0),
    )(result)


def solution(mesh):
    placed = P("wide", "narrow")
    return jax.shard_map(
        shards, mesh=mesh, in_specs=(placed, placed, placed), out_specs=placed, check_vma=False
    )
```

time: 143 us -> 70.7 us (0.49)
  blocking collectives: 73.7 us -> 0 us
  Pallas kernels: 0 us -> 68 us
  waiting for transfers between devices: 28.5 us -> 0 us
  between operations: 13.4 us -> 0.01 us
  matrix products: 11.4 us -> 0 us
  local copies, waits for them, and re-layouts: 13.2 us -> 2.6 us
  other arithmetic: 2.04 us -> 0 us
    pallas_call x0 -> x2, Pallas kernels: none -> 68 us  [the longest x1 64.6 us: shards(): pl.pallas_call(kernel, out_shape=jax.ShapeDtypeStruct((rows, columns), jn...]
    all_to_all x2 -> x0, blocking collectives: 60.2 us -> none  [sent_to_all(): lax.all_to_all(jnp.broadcast_to(shard[None], (length, *shard.shape)), axi...]
    all_gather x2 -> x0, waiting for transfers between devices: 28.5 us -> none  [gather_in_order(): tiles = lax.all_gather(tiles, axes[k], axis=0, tiled=True)]
    all_gather x1 -> x0, blocking collectives: 13.5 us -> none  [gather_in_order(): tiles = lax.all_gather(tiles, axes[k], axis=0, tiled=True)]
    dot_general x1 -> x0, matrix products: 11.4 us -> none  [shards(): jnp.dot(whole_rows, gathered_by_axis(integrals, WIDE, (1, 0, 2), 0), pref...]
    transpose x2 -> x0, local copies, waits for them, and re-layouts: 9.38 us -> none  [the longest x1 6.52 us: laid_out(): tiles = jnp.moveaxis(tiles, 0, dim)]
    all_to_all x1 -> x0, local copies, waits for them, and re-layouts: 2.32 us -> none  [sent_to_all(): lax.all_to_all(jnp.broadcast_to(shard[None], (length, *shard.shape)), axi...]
    unnamed x2 -> x6, local copies, waits for them, and re-layouts: 0.58 us -> 2.6 us
  transfers between devices with their start and end apart: 2 -> 0, of which waited for: 1 -> 0; matrix products, arithmetic and copies ran while one was open for 8% -> 0% of each run, Pallas kernels for 0% -> 0%
where the time goes in v1:
time: 70.7 us; the launch traced here: 70.6 us
  Pallas kernels  68 us (96%)
  local copies, waits for them, and re-layouts  2.6 us (4%)
    pallas_call x1, Pallas kernels, shards(): pl.pallas_call(kernel, out_shape=jax.ShapeDtypeStruct((rows, columns), jn...  64.6 us
    pallas_call x1, Pallas kernels, shards(): pl.pallas_call(write_out, out_shape=jax.ShapeDtypeStruct(result.shape, re...  3.37 us
    unnamed x6, local copies, waits for them, and re-layouts  2.6 us

profile of v1, /device:TPU:1, one launch (start us, length us, event | category | flops | bytes accessed | tf_op | source)
XLA Modules:
  0.0 70.6 jit_solution(14349942327616935448)
XLA Ops:
  0.0 0.0 copy-start
  0.0 1.0 %copy-done = bf16[2048,128]{1,0:T(8,128)(2,1)S(1)} copy-done((bf16[2048,128]{1,0:T(8,128)(2,1)S(1)}, bf16[2048,128]{1,0:T(8,128)(2,1)}, u32[]{:S(2)}) %copy-start) | copy-done | bytes 524312
  1.0 0.0 copy-start.1
  1.0 0.9 %copy-done.1 = bf16[32,2048]{1,0:T(8,128)(2,1)S(1)} copy-done((bf16[32,2048]{1,0:T(8,128)(2,1)S(1)}, bf16[32,2048]{1,0:T(8,128)(2,1)}, u32[]{:S(2)}) %copy-start.1) | copy-done | bytes 131096
  1.9 0.0 copy-start.2
  1.9 0.7 copy-done.2
  2.6 64.6 %shard_map.37.from_ref = bf16[2048,2048]{1,0:T(8,128)(2,1)S(1)} custom-call(s32[1,16]{1,0:T(1,128)S(1)} %bitcast.1, bf16[2048,128]{1,0:T(8,128)(2,1)S(1)} %copy-done, bf16[32,2048]{1,0:T(8,128)(2,1)S(1)} %copy-done.1), custom_call_target="tpu_custom_call" | custom-call | flops 8589934592 | bytes 8388608 | tf_op jit(solution)/shard_map/pallas_call | solution.py:283
  67.2 3.4 %shard_map.38 = bf16[2048,2048]{1,0:T(8,128)(2,1)} custom-call(bf16[2048,2048]{1,0:T(8,128)(2,1)S(1)} %shard_map.37.from_ref), custom_call_target="tpu_custom_call" | custom-call | bytes 8388608 | tf_op jit(solution)/shard_map/pallas_call | solution.py:312
Async XLA Ops:
  0.0 1.0 %copy-start = (bf16[2048,128]{1,0:T(8,128)(2,1)S(1)}, bf16[2048,128]{1,0:T(8,128)(2,1)}, u32[]{:S(2)}) copy-start(bf16[2048,128]{1,0:T(8,128)(2,1)} %a_ref.1) | copy-start | bytes 1572868
  1.0 0.9 %copy-start.1 = (bf16[32,2048]{1,0:T(8,128)(2,1)S(1)}, bf16[32,2048]{1,0:T(8,128)(2,1)}, u32[]{:S(2)}) copy-start(bf16[32,2048]{1,0:T(8,128)(2,1)} %b_ref.1) | copy-start | bytes 393220
  1.9 0.7 copy-start.2

commit v2 on v1

--- a/solution.py
+++ b/solution.py
@@ -13,11 +13,15 @@
 RING = 4
 CORES = 2
 CHUNK = 128
+BLOCK = 256
+TALL = 512
 COLS = 512
 WRITES = 8
 
 
-def kernel(mask_ref, a_ref, b_ref, out_ref, a_in, a_all, b_all, local, za, ca, up, down, side, zb, sb):
+def kernel(
+    mask_hbm, a_ref, b_ref, out_ref, mask_ref, a_in, a_all, b_all, total, local, za, ca, up, down, side, zb, sb, ready
+):
     wide, narrow = lax.axis_index("wide"), lax.axis_index("narrow")
     zl, core = narrow // CORES, narrow % CORES
     x, zh, y = wide // (2 * RING), (wide // RING) % 2, wide % RING
@@ -25,6 +29,9 @@
     depth = b_ref.shape[0]
     half = depth // 2
     chunks = rows // CHUNK
+    near = jnp.where(zl < LINE // 2, 0, LINE // 2)
+    middle = jnp.where(zl < LINE // 2, LINE // 2, LINE // 2 - 1)
+    late = jnp.where(zl < LINE // 2, LINE - 1, 0)
 
     def wide_of(layer, first, second):
         px = (x + (1 - core) * first + core * second) % RING
@@ -36,8 +43,10 @@
 
     take_b = pltpu.make_async_copy(b_ref, b_all.at[pl.ds(wide * depth, depth)], local.at[0])
     take_a = pltpu.make_async_copy(a_ref, a_in, local.at[1])
+    take_mask = pltpu.make_async_copy(mask_hbm, mask_ref, local.at[2])
+    take_a.start()
+    take_mask.start()
     take_b.start()
-    take_a.start()
 
     barrier = pltpu.get_barrier_semaphore()
 
@@ -46,8 +55,12 @@
 
     for first, second in ((1, 0), (3, 0), (0, 1), (0, 3)):
         greet((wide_of(0, first, second), narrow))
-    greet((wide_of(1, 0, 0), narrow))
     greet(other)
+    peer = (wide_of(1, 0, 0), narrow)
+
+    @pl.when(zh == 0)
+    def _():
+        greet(peer)
 
     @pl.when(zl < LINE - 1)
     def _():
@@ -58,10 +71,8 @@
         greet(below)
 
     inner = jnp.where((zl > 0) & (zl < LINE - 1), 1, 0)
-    pl.semaphore_wait(barrier, 7 + inner)
-    take_b.wait()
-
-    sent = []
+    pl.semaphore_wait(barrier, 6 + inner + zh)
+
 
     def b_part(layer, first, second, part):
         base = wide_of(layer, first, second) * depth
@@ -74,7 +85,7 @@
         return pltpu.make_async_remote_copy(
             where,
             where,
-            sb.at[len(sent)],
+            sb.at[0],
             zb.at[label[0], label[1] % RING, label[2] % RING, part or 0],
             device_id=(wide_of(*to), narrow),
             device_id_type=MESH,
@@ -82,9 +93,7 @@
 
     def b_send(layer, first, second, part, step):
         df, ds = step
-        copy = b_copy(layer, first, second, part, (0, df, ds), (layer, first - df, second - ds))
-        copy.start()
-        sent.append(copy)
+        b_copy(layer, first, second, part, (0, df, ds), (layer, first - df, second - ds)).start()
 
     def b_wait(layer, first, second, part):
         where = b_part(layer, first, second, part)
@@ -129,32 +138,35 @@
             b_wait(layer, first, 2, 1)
 
     swap = b_copy(0, 0, 0, None, (1, 0, 0), (1, 0, 0))
-    swap.start()
-    sent.append(swap)
-    b_begin(0)
+    take_b.wait()
+
+    @pl.when(zh == 1)
+    def _():
+        pl.semaphore_signal(ready, inc=1, device_id=peer, device_id_type=MESH)
+        swap.start()
 
     def a_copy(source, r, send, recv, device):
         where = a_all.at[source, core, pl.ds(pl.multiple_of(r * CHUNK, CHUNK), CHUNK)]
         return pltpu.make_async_remote_copy(
-            where, where, send.at[source, r], recv.at[source, r], device_id=device, device_id_type=MESH
+            where, where, send.at[source], recv, device_id=device, device_id_type=MESH
         )
 
     def over(source, r):
-        return a_copy(source, r, side, ca, other)
+        return a_copy(source, r, side, ca.at[source, jnp.where(source == late, r, 0)], other)
 
     def upward(source, r):
-        return a_copy(source, r, up, za, above)
+        return a_copy(source, r, up, za.at[source, r], above)
 
     def downward(source, r):
-        return a_copy(source, r, down, za, below)
-
-    def from_other(source, r):
-        where = a_all.at[source, 1 - core, pl.ds(pl.multiple_of(r * CHUNK, CHUNK), CHUNK)]
+        return a_copy(source, r, down, za.at[source, r], below)
+
+    def from_other(where, r, source):
         pltpu.make_async_remote_copy(
-            where, where, side.at[source, r], ca.at[source, r], device_id=other, device_id_type=MESH
+            where, where, side.at[source], ca.at[source, r], device_id=other, device_id_type=MESH
         ).wait_recv()
 
     take_a.wait()
+    take_mask.wait()
 
     def own(r, _):
         span = pl.ds(pl.multiple_of(r * CHUNK, CHUNK), CHUNK)
@@ -202,64 +214,134 @@
 
         lax.fori_loop(start * chunks // 16, stop * chunks // 16, body, 0)
 
+    def tile(place, c, span):
+        return a_all[place, c, span, :]
+
+    def deep(place, c):
+        return pl.ds(pl.multiple_of((place * CORES + c) * width, width), width)
+
+    def multiply(places, span, start):
+        left = jnp.concatenate([tile(place, c, span) for place, c in places], axis=1)
+        right = jnp.concatenate([b_all[deep(place, c), start : start + COLS] for place, c in places], axis=0)
+        return jnp.dot(left, right, preferred_element_type=jnp.float32)
+
+    def first_part(q):
+        span = pl.ds(pl.multiple_of(q * TALL, TALL), TALL)
+        for start in range(0, out_ref.shape[1], COLS):
+            total[span, start : start + COLS] = multiply([(near, zh), (near + 1, zh)], span, start)
+
+    def second_part(q):
+        span = pl.ds(pl.multiple_of(q * TALL, TALL), TALL)
+        places = [(near, 1 - zh), (near + 1, 1 - zh), (middle, 0), (middle, 1)]
+        for start in range(0, out_ref.shape[1], COLS):
+            total[span, start : start + COLS] += multiply(places, span, start)
+
+    talls = rows // TALL
+
+    def first_parts(start, stop):
+        first_chunk, last_chunk = start, stop
+
+        def body(q, _):
+            first_part(q)
+            per = (last_chunk - first_chunk) // talls
+            for i in range(per):
+                forward(2, first_chunk + q * per + i)
+            return 0
+
+        lax.fori_loop(0, talls, body, 0)
+
+    def second_parts():
+        per = chunks // 2 // talls
+
+        def body(q, _):
+            second_part(q)
+            for i in range(per):
+                forward(3, q * per + i)
+            return 0
+
+        lax.fori_loop(0, talls, body, 0)
+
+    b_begin(0)
     b_near(0)
+    b_turn(0, 0)
+
+    @pl.when(zh == 0)
+    def _():
+        pl.semaphore_wait(ready, 1)
+        swap.start()
+
     b_far(0)
-    for first in range(RING):
-        b_turn(0, first)
-    forwards(1, 0, 8)
+    b_turn(0, 3)
+    forwards(1, 0, 6)
+    b_turn(0, 1)
+    forwards(1, 6, 10)
+    b_turn(0, 2)
+    forwards(1, 10, 14)
     b_wait(1, 0, 0, None)
     b_begin(1)
-    forwards(1, 8, 10)
+    forwards(1, 14, 16)
     b_near(1)
-    forwards(1, 10, 12)
+    b_turn(1, 0)
+    forwards(2, 0, 2)
     b_far(1)
-    forwards(1, 12, 16)
-    for first in range(RING):
-        b_turn(1, first)
+    b_turn(1, 3)
+    forwards(2, 2, 5)
+    b_turn(1, 1)
+    forwards(2, 5, 8)
+    b_turn(1, 2)
     b_end(0)
+    for i in range(2):
+        from_other(a_all.at[near + i, 1 - core], 0, near + i)
+    first_parts(8, 16)
     b_end(1)
-    forwards(2, 0, 16)
-
-    def product(r):
-        span = pl.ds(pl.multiple_of(r * CHUNK, CHUNK), CHUNK)
-        for source in range(LINE):
-            from_other(source, r)
-        left = jnp.concatenate([a_all[s, c, span, :] for s in range(LINE) for c in range(CORES)], axis=1)
+    from_other(a_all.at[middle, 1 - core], 0, middle)
+    second_parts()
+
+    def final(q):
+        for i in range(BLOCK // CHUNK):
+            r = q * (BLOCK // CHUNK) + i
+            from_other(a_all.at[late, 1 - core, pl.ds(pl.multiple_of(r * CHUNK, CHUNK), CHUNK)], r, late)
+        span = pl.ds(pl.multiple_of(q * BLOCK, BLOCK), BLOCK)
         for start in range(0, out_ref.shape[1], COLS):
-            out_ref[span, start : start + COLS] = jnp.dot(
-                left, b_all[:, start : start + COLS], preferred_element_type=jnp.float32
+            out_ref[span, start : start + COLS] = (
+                total[span, start : start + COLS] + multiply([(late, 0), (late, 1)], span, start)
             ).astype(out_ref.dtype)
 
-    def last(r, _):
-        forward(3, r)
-
-        @pl.when(r > 0)
-        def _():
-            product(r - 1)
-
+    blocks = rows // BLOCK
+
+    def last_part(r, _):
+        for i in range(chunks // 2 // blocks):
+            forward(3, chunks // 2 + r * (chunks // 2 // blocks) + i)
+        final(r)
         return 0
 
-    lax.fori_loop(0, chunks, last, 0)
-    product(chunks - 1)
-
-    for copy in sent:
-        copy.wait_send()
-
-    def finish(i, _):
-        source, r = i // chunks, i % chunks
-        over(source, r).wait_send()
+    lax.fori_loop(0, blocks, last_part, 0)
+
+    everything = b_all.at[pl.ds(0, b_all.shape[0] - depth)]
+    pltpu.make_async_remote_copy(
+        everything, everything, sb.at[0], zb.at[0, 0, 0, 0], device_id=other, device_id_type=MESH
+    ).wait_send()
+
+    def finish(source, _):
+        def sent(sem):
+            where = a_all.at[source, core]
+            pltpu.make_async_remote_copy(
+                where, where, sem.at[source], za.at[0, 0], device_id=other, device_id_type=MESH
+            ).wait_send()
+
+        sent(side)
 
         @pl.when((source <= zl) & (zl < LINE - 1))
         def _():
-            upward(source, r).wait_send()
+            sent(up)
 
         @pl.when((source >= zl) & (zl > 0))
         def _():
-            downward(source, r).wait_send()
+            sent(down)
 
         return 0
 
-    lax.fori_loop(0, LINE * chunks, finish, 0)
+    lax.fori_loop(0, LINE, finish, 0)
 
 
 def write_out(from_ref, to_ref, sem):
@@ -284,31 +366,34 @@
         kernel,
         out_shape=jax.ShapeDtypeStruct((rows, columns), jnp.bfloat16),
         in_specs=[
-            pl.BlockSpec(memory_space=pltpu.SMEM),
+            pl.BlockSpec(memory_space=pltpu.HBM),
             pl.BlockSpec(memory_space=pltpu.HBM),
             pl.BlockSpec(memory_space=pltpu.HBM),
         ],
         out_specs=pl.BlockSpec(memory_space=pltpu.VMEM),
         scratch_shapes=[
+            pltpu.SMEM((1, rows // VB), jnp.int32),
             pltpu.VMEM((rows, width), jnp.bfloat16),
             pltpu.VMEM((LINE, CORES, rows, width), jnp.bfloat16),
             pltpu.VMEM((deep, columns), jnp.bfloat16),
-            dma((2,)),
+            pltpu.VMEM((rows, columns), jnp.float32),
+            dma((3,)),
             dma((LINE, chunks)),
             dma((LINE, chunks)),
-            dma((LINE, chunks)),
-            dma((LINE, chunks)),
-            dma((LINE, chunks)),
+            dma((LINE,)),
+            dma((LINE,)),
+            dma((LINE,)),
             dma((2, RING, RING, 2)),
-            dma((48,)),
+            dma((1,)),
+            pltpu.SemaphoreType.REGULAR,
         ],
         compiler_params=pltpu.CompilerParams(
-            collective_id=0, has_side_effects=True, vmem_limit_bytes=32 * 2**20
+            collective_id=0, has_side_effects=True, vmem_limit_bytes=40 * 2**20
         ),
         cost_estimate=pl.CostEstimate(
             flops=2 * rows * columns * deep, bytes_accessed=2 * rows * columns, transcendentals=0
         ),
-    )(pair_mask.reshape(1, -1), amplitudes, integrals)
+    )(*[pltpu.with_memory_space_constraint(v, pltpu.HBM) for v in (pair_mask.reshape(1, -1), amplitudes, integrals)])
     return pl.pallas_call(
         write_out,
         out_shape=jax.ShapeDtypeStruct(result.shape, result.dtype),

time: 70.7 us -> 56.3 us (0.80)
  the two profiles are of different devices: /device:TPU:1 before, /device:TPU:225 now
where the time goes in v2:
time: 56.3 us; the launch traced here: 56.2 us
  Pallas kernels  56.2 us (100%)
    pallas_call x1, Pallas kernels, shards(): pl.pallas_call(kernel, out_shape=jax.ShapeDtypeStruct((rows, columns), jn...  52.8 us
    pallas_call x1, Pallas kernels, shards(): pl.pallas_call(write_out, out_shape=jax.ShapeDtypeStruct(result.shape, re...  3.37 us

profile of v2, /device:TPU:225, one launch (start us, length us, event | category | flops | bytes accessed | tf_op | source)
XLA Modules:
  0.0 56.2 jit_solution(5224459439863419172)
XLA Ops:
  0.0 52.8 %shard_map.37.from_ref = bf16[2048,2048]{1,0:T(8,128)(2,1)S(1)} custom-call(s32[1,16]{1,0:T(1,128)} %bitcast.1, bf16[2048,128]{1,0:T(8,128)(2,1)} %a_ref.1, bf16[32,2048]{1,0:T(8,128)(2,1)} %b_ref.1), custom_call_target="tpu_custom_call" | custom-call | flops 8589934592 | bytes 8388608 | tf_op jit(solution)/shard_map/pallas_call | solution.py:365
  52.8 3.4 %shard_map.38 = bf16[2048,2048]{1,0:T(8,128)(2,1)} custom-call(bf16[2048,2048]{1,0:T(8,128)(2,1)S(1)} %shard_map.37.from_ref), custom_call_target="tpu_custom_call" | custom-call | bytes 8388608 | tf_op jit(solution)/shard_map/pallas_call | solution.py:397

commit v3 on v2

--- a/solution.py
+++ b/solution.py
@@ -15,12 +15,32 @@
 CHUNK = 128
 BLOCK = 256
 TALL = 512
+REST = 512
 COLS = 512
-WRITES = 8
 
 
 def kernel(
-    mask_hbm, a_ref, b_ref, out_ref, mask_ref, a_in, a_all, b_all, total, local, za, ca, up, down, side, zb, sb, ready
+    mask_hbm,
+    a_ref,
+    b_ref,
+    out_ref,
+    total_rest,
+    a_rest,
+    b_rest,
+    mask_ref,
+    a_in,
+    a_all,
+    b_all,
+    total,
+    local,
+    za,
+    ca,
+    up,
+    down,
+    side,
+    zb,
+    sb,
+    ready,
 ):
     wide, narrow = lax.axis_index("wide"), lax.axis_index("narrow")
     zl, core = narrow // CORES, narrow % CORES
@@ -106,44 +126,48 @@
             device_id_type=MESH,
         ).wait_recv()
 
-    def b_begin(layer):
-        for step in ((1, 0), (3, 0), (0, 1), (0, 3)):
-            b_send(layer, 0, 0, None, step)
-
-    def b_near(layer):
-        b_wait(layer, 3, 0, None)
-        b_send(layer, 3, 0, 0, (1, 0))
-        b_send(layer, 3, 0, None, (0, 1))
-        b_send(layer, 3, 0, None, (0, 3))
-        b_wait(layer, 1, 0, None)
-        b_send(layer, 1, 0, 1, (3, 0))
-        b_send(layer, 1, 0, None, (0, 1))
-        b_send(layer, 1, 0, None, (0, 3))
-
-    def b_far(layer):
-        b_wait(layer, 2, 0, 0)
-        b_wait(layer, 2, 0, 1)
-        b_send(layer, 2, 0, None, (0, 1))
-        b_send(layer, 2, 0, None, (0, 3))
+    def b_both(layer, first, part):
+        b_send(layer, first, 0, part, (0, 1))
+        b_send(layer, first, 0, part, (0, 3))
+
+    def b_begin(layer, part):
+        b_send(layer, 0, 0, part, (1, 0))
+        b_send(layer, 0, 0, part, (3, 0))
+        b_both(layer, 0, part)
+
+    def b_near(layer, part):
+        ahead, behind = ((3, 1), (1, 3))[part]
+        b_wait(layer, ahead, 0, part)
+        b_send(layer, ahead, 0, part, (behind, 0))
+        b_both(layer, ahead, part)
+        b_wait(layer, behind, 0, part)
+        b_both(layer, behind, part)
+
+    def b_far(layer, part):
+        b_wait(layer, 2, 0, part)
+        b_both(layer, 2, part)
 
     def b_turn(layer, first):
-        b_wait(layer, first, 3, None)
+        b_wait(layer, first, 3, 0)
         b_send(layer, first, 3, 0, (0, 1))
-        b_wait(layer, first, 1, None)
+        b_wait(layer, first, 1, 1)
         b_send(layer, first, 1, 1, (0, 3))
 
     def b_end(layer):
         for first in range(RING):
+            b_wait(layer, first, 3, 1)
+            b_wait(layer, first, 1, 0)
             b_wait(layer, first, 2, 0)
             b_wait(layer, first, 2, 1)
 
-    swap = b_copy(0, 0, 0, None, (1, 0, 0), (1, 0, 0))
+    swaps = [b_copy(0, 0, 0, part, (1, 0, 0), (1, 0, 0)) for part in (0, 1)]
     take_b.wait()
 
     @pl.when(zh == 1)
     def _():
         pl.semaphore_signal(ready, inc=1, device_id=peer, device_id_type=MESH)
-        swap.start()
+        for swap in swaps:
+            swap.start()
 
     def a_copy(source, r, send, recv, device):
         where = a_all.at[source, core, pl.ds(pl.multiple_of(r * CHUNK, CHUNK), CHUNK)]
@@ -184,6 +208,8 @@
         over(zl, r).start()
         return 0
 
+    b_begin(0, 0)
+    b_begin(0, 1)
     lax.fori_loop(0, chunks, own, 0)
 
     def forward(distance, r):
@@ -225,97 +251,128 @@
         right = jnp.concatenate([b_all[deep(place, c), start : start + COLS] for place, c in places], axis=0)
         return jnp.dot(left, right, preferred_element_type=jnp.float32)
 
-    def first_part(q):
-        span = pl.ds(pl.multiple_of(q * TALL, TALL), TALL)
-        for start in range(0, out_ref.shape[1], COLS):
-            total[span, start : start + COLS] = multiply([(near, zh), (near + 1, zh)], span, start)
-
-    def second_part(q):
-        span = pl.ds(pl.multiple_of(q * TALL, TALL), TALL)
+    columns = out_ref.shape[1]
+    talls = total.shape[0] // TALL
+    rest_talls = REST // TALL
+
+    def first_part(q, into, skip):
+        span = pl.ds(pl.multiple_of((q + skip) * TALL, TALL), TALL)
+        here = pl.ds(pl.multiple_of(q * TALL, TALL), TALL)
+        for start in range(0, columns, COLS):
+            into[here, start : start + COLS] = multiply([(near, zh), (near + 1, zh)], span, start)
+
+    def second_part(q, into, skip):
+        span = pl.ds(pl.multiple_of((q + skip) * TALL, TALL), TALL)
+        here = pl.ds(pl.multiple_of(q * TALL, TALL), TALL)
         places = [(near, 1 - zh), (near + 1, 1 - zh), (middle, 0), (middle, 1)]
-        for start in range(0, out_ref.shape[1], COLS):
-            total[span, start : start + COLS] += multiply(places, span, start)
-
-    talls = rows // TALL
-
-    def first_parts(start, stop):
-        first_chunk, last_chunk = start, stop
+        for start in range(0, columns, COLS):
+            into[here, start : start + COLS] += multiply(places, span, start)
+
+    def parts(part, distance, first_chunk, last_chunk):
+        per = (last_chunk - first_chunk) // (talls + rest_talls)
 
         def body(q, _):
-            first_part(q)
-            per = (last_chunk - first_chunk) // talls
+            part(q, total, 0)
             for i in range(per):
-                forward(2, first_chunk + q * per + i)
+                forward(distance, first_chunk + q * per + i)
             return 0
 
+        def rest_body(q, _):
+            part(q, total_rest, talls)
+            for i in range(per):
+                forward(distance, first_chunk + (talls + q) * per + i)
+            return 0
+
         lax.fori_loop(0, talls, body, 0)
-
-    def second_parts():
-        per = chunks // 2 // talls
-
-        def body(q, _):
-            second_part(q)
-            for i in range(per):
-                forward(3, q * per + i)
-            return 0
-
-        lax.fori_loop(0, talls, body, 0)
-
-    b_begin(0)
-    b_near(0)
+        lax.fori_loop(0, rest_talls, rest_body, 0)
+
+    def slice_of(q):
+        if q < talls:
+            first_part(q, total, 0)
+        else:
+            first_part(q - talls, total_rest, talls)
+
+    b_near(0, 0)
+    b_near(0, 1)
     b_turn(0, 0)
 
     @pl.when(zh == 0)
     def _():
         pl.semaphore_wait(ready, 1)
-        swap.start()
-
-    b_far(0)
+        for swap in swaps:
+            swap.start()
+
+    b_far(0, 0)
+    b_far(0, 1)
     b_turn(0, 3)
     forwards(1, 0, 6)
     b_turn(0, 1)
     forwards(1, 6, 10)
     b_turn(0, 2)
-    forwards(1, 10, 14)
-    b_wait(1, 0, 0, None)
-    b_begin(1)
+    forwards(1, 10, 12)
+    b_wait(1, 0, 0, 0)
+    b_begin(1, 0)
+    forwards(1, 12, 14)
+    b_wait(1, 0, 0, 1)
+    b_begin(1, 1)
+    b_near(1, 0)
     forwards(1, 14, 16)
-    b_near(1)
-    b_turn(1, 0)
-    forwards(2, 0, 2)
-    b_far(1)
-    b_turn(1, 3)
-    forwards(2, 2, 5)
-    b_turn(1, 1)
-    forwards(2, 5, 8)
-    b_turn(1, 2)
+    b_near(1, 1)
     b_end(0)
     for i in range(2):
         from_other(a_all.at[near + i, 1 - core], 0, near + i)
-    first_parts(8, 16)
+    b_far(1, 0)
+    slice_of(0)
+    b_turn(1, 0)
+    b_far(1, 1)
+    slice_of(1)
+    forwards(2, 0, 2)
+    b_turn(1, 3)
+    slice_of(2)
+    forwards(2, 2, 5)
+    b_turn(1, 1)
+    slice_of(3)
+    forwards(2, 5, 8)
+    b_turn(1, 2)
+    forwards(2, 8, 16)
     b_end(1)
     from_other(a_all.at[middle, 1 - core], 0, middle)
-    second_parts()
+    b_rest[...] = b_all[pl.ds(pl.multiple_of(late * CORES * width, CORES * width), CORES * width)]
+    parts(second_part, 3, 0, 8)
+
+    def arrive(start, stop):
+        def body(r, _):
+            from_other(a_all.at[late, 1 - core, pl.ds(pl.multiple_of(r * CHUNK, CHUNK), CHUNK)], r, late)
+            return 0
+
+        lax.fori_loop(start, stop, body, 0)
 
     def final(q):
-        for i in range(BLOCK // CHUNK):
-            r = q * (BLOCK // CHUNK) + i
-            from_other(a_all.at[late, 1 - core, pl.ds(pl.multiple_of(r * CHUNK, CHUNK), CHUNK)], r, late)
         span = pl.ds(pl.multiple_of(q * BLOCK, BLOCK), BLOCK)
-        for start in range(0, out_ref.shape[1], COLS):
+        for start in range(0, columns, COLS):
             out_ref[span, start : start + COLS] = (
                 total[span, start : start + COLS] + multiply([(late, 0), (late, 1)], span, start)
             ).astype(out_ref.dtype)
 
-    blocks = rows // BLOCK
-
-    def last_part(r, _):
-        for i in range(chunks // 2 // blocks):
-            forward(3, chunks // 2 + r * (chunks // 2 // blocks) + i)
-        final(r)
+    blocks = total.shape[0] // BLOCK
+    per = BLOCK // CHUNK
+
+    def last_part(q, _):
+        forward(3, chunks // 2 + q)
+        arrive(q * per, (q + 1) * per)
+        final(q)
         return 0
 
     lax.fori_loop(0, blocks, last_part, 0)
+
+    def last_forward(r, _):
+        forward(3, r)
+        return 0
+
+    lax.fori_loop(chunks // 2 + blocks, chunks, last_forward, 0)
+    arrive(blocks * per, chunks)
+    for c in range(CORES):
+        a_rest[:, c * width : (c + 1) * width] = a_all[late, c, pl.ds(rows - REST, REST), :]
 
     everything = b_all.at[pl.ds(0, b_all.shape[0] - depth)]
     pltpu.make_async_remote_copy(
@@ -344,14 +401,26 @@
     lax.fori_loop(0, LINE, finish, 0)
 
 
-def write_out(from_ref, to_ref, sem):
-    size = from_ref.shape[0] // WRITES
-    copies = [
-        pltpu.make_async_copy(from_ref.at[pl.ds(i * size, size)], to_ref.at[pl.ds(i * size, size)], sem.at[i])
-        for i in range(WRITES)
-    ]
-    for copy in copies:
+def finish_rows(done_ref, total_ref, a_ref, b_ref, to_ref, last, sem):
+    size, done = BLOCK, done_ref.shape[0]
+    copies = []
+
+    def send(where, row):
+        copy = pltpu.make_async_copy(where, to_ref.at[pl.ds(row, size)], sem.at[len(copies)])
         copy.start()
+        copies.append(copy)
+
+    for row in range(0, done, size):
+        send(done_ref.at[pl.ds(row, size)], row)
+    for row in range(0, last.shape[0], size):
+        for start in range(0, last.shape[1], COLS):
+            last[row : row + size, start : start + COLS] = (
+                total_ref[row : row + size, start : start + COLS]
+                + jnp.dot(
+                    a_ref[row : row + size], b_ref[:, start : start + COLS], preferred_element_type=jnp.float32
+                )
+            ).astype(last.dtype)
+        send(last.at[pl.ds(row, size)], done + row)
     for copy in copies:
         copy.wait()
 
@@ -362,21 +431,26 @@
     deep = depth * 2 * RING * RING
     chunks = rows // CHUNK
     dma = pltpu.SemaphoreType.DMA
-    result = pl.pallas_call(
+    held = pl.pallas_call(
         kernel,
-        out_shape=jax.ShapeDtypeStruct((rows, columns), jnp.bfloat16),
+        out_shape=[
+            jax.ShapeDtypeStruct((rows - REST, columns), jnp.bfloat16),
+            jax.ShapeDtypeStruct((REST, columns), jnp.float32),
+            jax.ShapeDtypeStruct((REST, CORES * width), jnp.bfloat16),
+            jax.ShapeDtypeStruct((CORES * width, columns), jnp.bfloat16),
+        ],
         in_specs=[
             pl.BlockSpec(memory_space=pltpu.HBM),
             pl.BlockSpec(memory_space=pltpu.HBM),
             pl.BlockSpec(memory_space=pltpu.HBM),
         ],
-        out_specs=pl.BlockSpec(memory_space=pltpu.VMEM),
+        out_specs=[pl.BlockSpec(memory_space=pltpu.VMEM)] * 4,
         scratch_shapes=[
             pltpu.SMEM((1, rows // VB), jnp.int32),
             pltpu.VMEM((rows, width), jnp.bfloat16),
             pltpu.VMEM((LINE, CORES, rows, width), jnp.bfloat16),
             pltpu.VMEM((deep, columns), jnp.bfloat16),
-            pltpu.VMEM((rows, columns), jnp.float32),
+            pltpu.VMEM((rows - REST, columns), jnp.float32),
             dma((3,)),
             dma((LINE, chunks)),
             dma((LINE, chunks)),
@@ -395,14 +469,16 @@
         ),
     )(*[pltpu.with_memory_space_constraint(v, pltpu.HBM) for v in (pair_mask.reshape(1, -1), amplitudes, integrals)])
     return pl.pallas_call(
-        write_out,
-        out_shape=jax.ShapeDtypeStruct(result.shape, result.dtype),
-        in_specs=[pl.BlockSpec(memory_space=pl.ANY)],
+        finish_rows,
+        out_shape=jax.ShapeDtypeStruct((rows, columns), jnp.bfloat16),
+        in_specs=[pl.BlockSpec(memory_space=pltpu.VMEM)] * 4,
         out_specs=pl.BlockSpec(memory_space=pltpu.HBM),
-        scratch_shapes=[dma((WRITES,))],
-        compiler_params=pltpu.CompilerParams(vmem_limit_bytes=2**20),
-        cost_estimate=pl.CostEstimate(flops=0, bytes_accessed=2 * rows * columns, transcendentals=0),
-    )(result)
+        scratch_shapes=[pltpu.VMEM((REST, columns), jnp.bfloat16), dma((rows // BLOCK,))],
+        compiler_params=pltpu.CompilerParams(vmem_limit_bytes=20 * 2**20),
+        cost_estimate=pl.CostEstimate(
+            flops=2 * REST * columns * CORES * width, bytes_accessed=2 * rows * columns, transcendentals=0
+        ),
+    )(*held)
 
 
 def solution(mesh):

time: 56.3 us -> 53.6 us (0.952)
  Pallas kernels: 56.2 us -> 53.5 us
    pallas_call x2, Pallas kernels: 56.2 us -> 53.5 us  [the longest x1 50.1 us: shards(): pl.pallas_call(kernel, out_shape=[jax.ShapeDtypeStruct((rows - REST, colu...]
where the time goes in v3:
time: 53.6 us; the launch traced here: 53.5 us
  Pallas kernels  53.5 us (100%)
    pallas_call x1, Pallas kernels, shards(): pl.pallas_call(kernel, out_shape=[jax.ShapeDtypeStruct((rows - REST, colu...  50.1 us
    pallas_call x1, Pallas kernels, shards(): pl.pallas_call(finish_rows, out_shape=jax.ShapeDtypeStruct((rows, columns...  3.37 us

profile of v3, /device:TPU:225, one launch (start us, length us, event | category | flops | bytes accessed | tf_op | source)
XLA Modules:
  0.0 53.5 jit_solution(4598775777987666688)
XLA Ops:
  0.0 50.1 %shard_map.37 = (bf16[1536,2048]{1,0:T(8,128)(2,1)S(1)}, f32[512,2048]{1,0:T(8,128)S(1)}, bf16[512,256]{1,0:T(8,128)(2,1)S(1)}, bf16[256,2048]{1,0:T(8,128)(2,1)S(1)}) custom-call(s32[1,16]{1,0:T(1,128)} %bitcast.1, bf16[2048,128]{1,0:T(8,128)(2,1)} %a_ref.1, bf16[32,2048]{1,0:T(8,128)(2,1)} %b_ref.1), custom_call_target="tpu_custom_call" | custom-call | flops 8589934592 | bytes 8388608 | tf_op jit(solution)/shard_map/pallas_call | solution.py:434
  50.2 3.4 %shard_map.38 = bf16[2048,2048]{1,0:T(8,128)(2,1)} custom-call(bf16[1536,2048]{1,0:T(8,128)(2,1)S(1)} %get-tuple-element.9.done_ref, f32[512,2048]{1,0:T(8,128)S(1)} %get-tuple-element.10.total_ref, bf16[512,256]{1,0:T(8,128)(2,1)S(1)} %get-tuple-element.11.a_ref, bf16[256,2048]{1,0:T(8,128)(2,1)S(1)} %get-tuple-element.12.b_ref), custom_call_target="tpu_custom_call" | custom-call | flops 536870912 | bytes 8388608 | tf_op jit(solution)/shard_map/pallas_call | solution.py:471

commit v4 on v3

--- a/solution.py
+++ b/solution.py
@@ -15,7 +15,8 @@
 CHUNK = 128
 BLOCK = 256
 TALL = 512
-REST = 512
+REST = 1024
+AHEAD = 6
 COLS = 512
 
 
@@ -210,7 +211,8 @@
 
     b_begin(0, 0)
     b_begin(0, 1)
-    lax.fori_loop(0, chunks, own, 0)
+    held_back = jnp.where((inner == 0) & (zh == 0), AHEAD, chunks)
+    lax.fori_loop(0, held_back, own, 0)
 
     def forward(distance, r):
         @pl.when(zl - distance >= 0)
@@ -302,6 +304,7 @@
         for swap in swaps:
             swap.start()
 
+    lax.fori_loop(held_back, chunks, own, 0)
     b_far(0, 0)
     b_far(0, 1)
     b_turn(0, 3)

time: 53.6 us -> 52.4 us (0.978)
  the two profiles are of different devices: /device:TPU:225 before, /device:TPU:1 now
where the time goes in v4:
time: 52.4 us; the launch traced here: 52.3 us
  Pallas kernels  52.3 us (100%)
    pallas_call x1, Pallas kernels, shards(): pl.pallas_call(kernel, out_shape=[jax.ShapeDtypeStruct((rows - REST, colu...  49 us
    pallas_call x1, Pallas kernels, shards(): pl.pallas_call(finish_rows, out_shape=jax.ShapeDtypeStruct((rows, columns...  3.37 us

profile of v4, /device:TPU:1, one launch (start us, length us, event | category | flops | bytes accessed | tf_op | source)
XLA Modules:
  0.0 52.3 jit_solution(420179540090503774)
XLA Ops:
  0.0 49.0 %shard_map.37 = (bf16[1024,2048]{1,0:T(8,128)(2,1)S(1)}, f32[1024,2048]{1,0:T(8,128)S(1)}, bf16[1024,256]{1,0:T(8,128)(2,1)S(1)}, bf16[256,2048]{1,0:T(8,128)(2,1)S(1)}) custom-call(s32[1,16]{1,0:T(1,128)} %bitcast.1, bf16[2048,128]{1,0:T(8,128)(2,1)} %a_ref.1, bf16[32,2048]{1,0:T(8,128)(2,1)} %b_ref.1), custom_call_target="tpu_custom_call" | custom-call | flops 8589934592 | bytes 8388608 | tf_op jit(solution)/shard_map/pallas_call | solution.py:437
  49.0 3.4 %shard_map.38 = bf16[2048,2048]{1,0:T(8,128)(2,1)} custom-call(bf16[1024,2048]{1,0:T(8,128)(2,1)S(1)} %get-tuple-element.9.done_ref, f32[1024,2048]{1,0:T(8,128)S(1)} %get-tuple-element.10.total_ref, bf16[1024,256]{1,0:T(8,128)(2,1)S(1)} %get-tuple-element.11.a_ref, bf16[256,2048]{1,0:T(8,128)(2,1)S(1)} %get-tuple-element.12.b_ref), custom_call_target="tpu_custom_call" | custom-call | flops 1073741824 | bytes 8388608 | tf_op jit(solution)/shard_map/pallas_call | solution.py:474

commit v5 on v4

--- a/solution.py
+++ b/solution.py
@@ -74,25 +74,47 @@
     def greet(device):
         pl.semaphore_signal(barrier, inc=1, device_id=device, device_id_type=MESH)
 
-    for first, second in ((1, 0), (3, 0), (0, 1), (0, 3)):
-        greet((wide_of(0, first, second), narrow))
+    peer = (wide_of(1, 0, 0), narrow)
+
+    def to_x(px):
+        return (((px + RING) % RING * 2 + zh) * RING + y, narrow)
+
+    def to_y(py):
+        return ((x * 2 + zh) * RING + (py + RING) % RING, narrow)
+
+    higher = (
+        (x < RING - 1, to_x(x + 1), 1),
+        (x == 0, to_x(RING - 1), 1),
+        (y < RING - 1, to_y(y + 1), 1),
+        (y == 0, to_y(RING - 1), 1),
+        (zl < LINE - 1, above, 0),
+        (zh == 0, peer, 2),
+    )
+    lower = (
+        (x > 0, to_x(x - 1), 1),
+        (x == RING - 1, to_x(0), 1),
+        (y > 0, to_y(y - 1), 1),
+        (y == RING - 1, to_y(0), 1),
+        (zl > 0, below, 0),
+        (zh == 1, peer, 2),
+    )
     greet(other)
-    peer = (wide_of(1, 0, 0), narrow)
-
-    @pl.when(zh == 0)
-    def _():
-        greet(peer)
-
-    @pl.when(zl < LINE - 1)
-    def _():
-        greet(above)
-
-    @pl.when(zl > 0)
-    def _():
-        greet(below)
-
+    for present, device, _ in higher:
+        pl.when(present)(functools.partial(greet, device))
+
+    def count(*conditions):
+        return sum(jnp.where(c, 1, 0) for c in conditions)
+
+    before = count(*(present for present, _, _ in lower))
+    pl.semaphore_wait(barrier, 1 + before)
+    for present, device, kind in lower:
+        pl.when(present)(
+            functools.partial(
+                pl.semaphore_signal, ready.at[kind], inc=1, device_id=device, device_id_type=MESH
+            )
+        )
     inner = jnp.where((zl > 0) & (zl < LINE - 1), 1, 0)
-    pl.semaphore_wait(barrier, 6 + inner + zh)
+    in_plane = count(*(present for present, _, kind in higher if kind == 1))
 
 
     def b_part(layer, first, second, part):
@@ -166,7 +188,6 @@
 
     @pl.when(zh == 1)
     def _():
-        pl.semaphore_signal(ready, inc=1, device_id=peer, device_id_type=MESH)
         for swap in swaps:
             swap.start()
 
@@ -198,10 +219,6 @@
         keep = mask_ref[0, r * CHUNK // VB].astype(jnp.float32)
         a_all[zl, core, span, :] = (a_in[span, :].astype(jnp.float32) * keep).astype(jnp.bfloat16)
 
-        @pl.when(zl < LINE - 1)
-        def _():
-            upward(zl, r).start()
-
         @pl.when(zl > 0)
         def _():
             downward(zl, r).start()
@@ -209,10 +226,30 @@
         over(zl, r).start()
         return 0
 
+    def own_up(r, _):
+        upward(zl, r).start()
+        return 0
+
+    def own_ups(start, stop):
+        @pl.when(zl < LINE - 1)
+        def _():
+            lax.fori_loop(start, stop, own_up, 0)
+
+    held_back = jnp.where((inner == 0) & (zh == 0), AHEAD, chunks)
+    lax.fori_loop(0, held_back, own, 0)
+
+    @pl.when(zl < LINE - 1)
+    def _():
+        pl.semaphore_wait(ready.at[0], 1)
+
+    own_ups(0, held_back)
+
+    @pl.when(in_plane > 0)
+    def _():
+        pl.semaphore_wait(ready.at[1], in_plane)
+
     b_begin(0, 0)
     b_begin(0, 1)
-    held_back = jnp.where((inner == 0) & (zh == 0), AHEAD, chunks)
-    lax.fori_loop(0, held_back, own, 0)
 
     def forward(distance, r):
         @pl.when(zl - distance >= 0)
@@ -300,11 +337,12 @@
 
     @pl.when(zh == 0)
     def _():
-        pl.semaphore_wait(ready, 1)
+        pl.semaphore_wait(ready.at[2], 1)
         for swap in swaps:
             swap.start()
 
     lax.fori_loop(held_back, chunks, own, 0)
+    own_ups(held_back, chunks)
     b_far(0, 0)
     b_far(0, 1)
     b_turn(0, 3)
@@ -462,7 +500,7 @@
             dma((LINE,)),
             dma((2, RING, RING, 2)),
             dma((1,)),
-            pltpu.SemaphoreType.REGULAR,
+            pltpu.SemaphoreType.REGULAR((3,)),
         ],
         compiler_params=pltpu.CompilerParams(
             collective_id=0, has_side_effects=True, vmem_limit_bytes=40 * 2**20

time: 52.4 us -> 51.5 us (0.983); the launches traced: 52.3 us -> 50.6 us
  Pallas kernels: 52.3 us -> 50.6 us
    pallas_call x1, Pallas kernels: 49 us -> 47.2 us  [shards(): pl.pallas_call(kernel, out_shape=[jax.ShapeDtypeStruct((rows - REST, colu...]
where the time goes in v5:
time: 51.5 us; the launch traced here: 50.6 us
  Pallas kernels  50.6 us (98%)
    pallas_call x1, Pallas kernels, shards(): pl.pallas_call(kernel, out_shape=[jax.ShapeDtypeStruct((rows - REST, colu...  47.2 us
    pallas_call x1, Pallas kernels, shards(): pl.pallas_call(finish_rows, out_shape=jax.ShapeDtypeStruct((rows, columns...  3.37 us

profile of v5, /device:TPU:1, one launch (start us, length us, event | category | flops | bytes accessed | tf_op | source)
XLA Modules:
  0.0 50.6 jit_solution(8486589165881042714)
XLA Ops:
  0.0 47.2 %shard_map.37 = (bf16[1024,2048]{1,0:T(8,128)(2,1)S(1)}, f32[1024,2048]{1,0:T(8,128)S(1)}, bf16[1024,256]{1,0:T(8,128)(2,1)S(1)}, bf16[256,2048]{1,0:T(8,128)(2,1)S(1)}) custom-call(s32[1,16]{1,0:T(1,128)} %bitcast.1, bf16[2048,128]{1,0:T(8,128)(2,1)} %a_ref.1, bf16[32,2048]{1,0:T(8,128)(2,1)} %b_ref.1), custom_call_target="tpu_custom_call" | custom-call | flops 8589934592 | bytes 8388608 | tf_op jit(solution)/shard_map/pallas_call | solution.py:475
  47.2 3.4 %shard_map.38 = bf16[2048,2048]{1,0:T(8,128)(2,1)} custom-call(bf16[1024,2048]{1,0:T(8,128)(2,1)S(1)} %get-tuple-element.9.done_ref, f32[1024,2048]{1,0:T(8,128)S(1)} %get-tuple-element.10.total_ref, bf16[1024,256]{1,0:T(8,128)(2,1)S(1)} %get-tuple-element.11.a_ref, bf16[256,2048]{1,0:T(8,128)(2,1)S(1)} %get-tuple-element.12.b_ref), custom_call_target="tpu_custom_call" | custom-call | flops 1073741824 | bytes 8388608 | tf_op jit(solution)/shard_map/pallas_call | solution.py:512

commit v6 on v5

--- a/solution.py
+++ b/solution.py
@@ -235,7 +235,8 @@
         def _():
             lax.fori_loop(start, stop, own_up, 0)
 
-    held_back = jnp.where((inner == 0) & (zh == 0), AHEAD, chunks)
+    ahead = jnp.where(inner == 0, AHEAD, jnp.where(zl == LINE // 2, 2 * AHEAD, chunks))
+    held_back = jnp.where(zh == 0, ahead, chunks)
     lax.fori_loop(0, held_back, own, 0)
 
     @pl.when(zl < LINE - 1)

time: 51.5 us -> 50.7 us (0.984); the launches traced: 50.6 us -> 50.6 us
  no operation moved by 1% of the time
where the time goes in v6:
time: 50.7 us; the launch traced here: 50.6 us
  Pallas kernels  50.6 us (100%)
    pallas_call x1, Pallas kernels, shards(): pl.pallas_call(kernel, out_shape=[jax.ShapeDtypeStruct((rows - REST, colu...  47.2 us
    pallas_call x1, Pallas kernels, shards(): pl.pallas_call(finish_rows, out_shape=jax.ShapeDtypeStruct((rows, columns...  3.37 us

profile of v6, /device:TPU:1, one launch (start us, length us, event | category | flops | bytes accessed | tf_op | source)
XLA Modules:
  0.0 50.6 jit_solution(16077566730643830836)
XLA Ops:
  0.0 47.2 %shard_map.37 = (bf16[1024,2048]{1,0:T(8,128)(2,1)S(1)}, f32[1024,2048]{1,0:T(8,128)S(1)}, bf16[1024,256]{1,0:T(8,128)(2,1)S(1)}, bf16[256,2048]{1,0:T(8,128)(2,1)S(1)}) custom-call(s32[1,16]{1,0:T(1,128)} %bitcast.1, bf16[2048,128]{1,0:T(8,128)(2,1)} %a_ref.1, bf16[32,2048]{1,0:T(8,128)(2,1)} %b_ref.1), custom_call_target="tpu_custom_call" | custom-call | flops 8589934592 | bytes 8388608 | tf_op jit(solution)/shard_map/pallas_call | solution.py:476
  47.2 3.4 %shard_map.38 = bf16[2048,2048]{1,0:T(8,128)(2,1)} custom-call(bf16[1024,2048]{1,0:T(8,128)(2,1)S(1)} %get-tuple-element.9.done_ref, f32[1024,2048]{1,0:T(8,128)S(1)} %get-tuple-element.10.total_ref, bf16[1024,256]{1,0:T(8,128)(2,1)S(1)} %get-tuple-element.11.a_ref, bf16[256,2048]{1,0:T(8,128)(2,1)S(1)} %get-tuple-element.12.b_ref), custom_call_target="tpu_custom_call" | custom-call | flops 1073741824 | bytes 8388608 | tf_op jit(solution)/shard_map/pallas_call | solution.py:513

commit v7 on v6

--- a/solution.py
+++ b/solution.py
@@ -12,11 +12,11 @@
 LINE = 4
 RING = 4
 CORES = 2
-CHUNK = 128
+CHUNK = 256
 BLOCK = 256
 TALL = 512
 REST = 1024
-AHEAD = 6
+AHEAD = 3
 COLS = 512
 
 
@@ -215,9 +215,11 @@
     take_mask.wait()
 
     def own(r, _):
-        span = pl.ds(pl.multiple_of(r * CHUNK, CHUNK), CHUNK)
-        keep = mask_ref[0, r * CHUNK // VB].astype(jnp.float32)
-        a_all[zl, core, span, :] = (a_in[span, :].astype(jnp.float32) * keep).astype(jnp.bfloat16)
+        for i in range(CHUNK // VB):
+            at = r * (CHUNK // VB) + i
+            span = pl.ds(pl.multiple_of(at * VB, VB), VB)
+            keep = mask_ref[0, at].astype(jnp.float32)
+            a_all[zl, core, span, :] = (a_in[span, :].astype(jnp.float32) * keep).astype(jnp.bfloat16)
 
         @pl.when(zl > 0)
         def _():
@@ -380,7 +382,7 @@
     b_end(1)
     from_other(a_all.at[middle, 1 - core], 0, middle)
     b_rest[...] = b_all[pl.ds(pl.multiple_of(late * CORES * width, CORES * width), CORES * width)]
-    parts(second_part, 3, 0, 8)
+    parts(second_part, 3, 0, chunks // 2)
 
     def arrive(start, stop):
         def body(r, _):

time: 50.7 us -> 50.2 us (level)
    pallas_call x1, Pallas kernels: 47.2 us -> 46.7 us  [shards(): pl.pallas_call(kernel, out_shape=[jax.ShapeDtypeStruct((rows - REST, colu...]
where the time goes in v7:
time: 50.2 us; the launch traced here: 50.1 us
  Pallas kernels  50.1 us (100%)
    pallas_call x1, Pallas kernels, shards(): pl.pallas_call(kernel, out_shape=[jax.ShapeDtypeStruct((rows - REST, colu...  46.7 us
    pallas_call x1, Pallas kernels, shards(): pl.pallas_call(finish_rows, out_shape=jax.ShapeDtypeStruct((rows, columns...  3.37 us

profile of v7, /device:TPU:1, one launch (start us, length us, event | category | flops | bytes accessed | tf_op | source)
XLA Modules:
  0.0 50.1 jit_solution(7143842706896182437)
XLA Ops:
  0.0 46.7 %shard_map.37 = (bf16[1024,2048]{1,0:T(8,128)(2,1)S(1)}, f32[1024,2048]{1,0:T(8,128)S(1)}, bf16[1024,256]{1,0:T(8,128)(2,1)S(1)}, bf16[256,2048]{1,0:T(8,128)(2,1)S(1)}) custom-call(s32[1,16]{1,0:T(1,128)} %bitcast.1, bf16[2048,128]{1,0:T(8,128)(2,1)} %a_ref.1, bf16[32,2048]{1,0:T(8,128)(2,1)} %b_ref.1), custom_call_target="tpu_custom_call" | custom-call | flops 8589934592 | bytes 8388608 | tf_op jit(solution)/shard_map/pallas_call | solution.py:478
  46.7 3.4 %shard_map.38 = bf16[2048,2048]{1,0:T(8,128)(2,1)} custom-call(bf16[1024,2048]{1,0:T(8,128)(2,1)S(1)} %get-tuple-element.9.done_ref, f32[1024,2048]{1,0:T(8,128)S(1)} %get-tuple-element.10.total_ref, bf16[1024,256]{1,0:T(8,128)(2,1)S(1)} %get-tuple-element.11.a_ref, bf16[256,2048]{1,0:T(8,128)(2,1)S(1)} %get-tuple-element.12.b_ref), custom_call_target="tpu_custom_call" | custom-call | flops 1073741824 | bytes 8388608 | tf_op jit(solution)/shard_map/pallas_call | solution.py:515
